TPU v7x, 32 devices: a whole 2x2x4 slice. The times are simulated.
32 devices in a mesh: ty: 8 (over z, y), tx: 4 (over x, core).
Axes of the slice: x: 2, y: 2, z: 4, core: 2. Of those that a mesh axis runs over, the one named last changes fastest.
Arguments:
- object_slices: float32 [2, 2, 4096, 2048], P(None, None, 'ty', 'tx'), may hold values from -1.1 to 1.1
- probe: float32 [2, 256, 256], replicated, may hold values from -4.2 to 4.2
- fresnel_phase: float32 [256, 256], replicated, may hold values from -3.140625 to 3.140625
- intensity: float32 [8, 4, 4, 256, 256], P('ty', 'tx'), may hold values from 0.05 to 2
- offsets: int32 [8, 4, 4, 2], P('ty', 'tx'), may hold values from -128 to 384, as said below
- counts: int32 [8, 4], replicated, may hold values from 1 to 4, as said below
Outputs:
- new_object: float32 [2, 2, 4096, 2048], P(None, None, 'ty', 'tx')
Inputs may be any that keep to these rules, and one draw needn't show every extreme that they name: The positions of a tile fill its slots 0 to counts - 1; some tile has 4. `offsets`: every window of 256 x 256 pixels lies inside the object.
All inputs are finite; a program needn't handle non-finite values.
Results may differ from a plain program's by a relative error of at most 0.0003.
Values sent between devices are 32-bit elements; how exact they have to be, the bound alone decides.
A program may use at most 128 MiB of HBM per device.

v0:
```python
import functools
import math

import jax
import jax.numpy as jnp
import ml_dtypes
import numpy as np
from jax import lax
from jax.experimental import pallas as pl
from jax.experimental.pallas import tpu as pltpu
from jax.sharding import PartitionSpec as P

STEP_SIZE = 0.25
F32 = jnp.float32
BF16 = jnp.bfloat16


def passed_along(value, axis, steps):
    count = lax.axis_size(axis)
    first, last = (max(0, -steps), min(count, count - steps))
    return lax.ppermute(value, axis, [(source, source + steps) for source in range(first, last)])


def basis_blocks(length):
    half = length // 2
    index = np.arange(length)
    turns = (index[:, None] * index[None, :]) % length
    angles = turns * (2.0 * math.pi / length)
    real = np.cos(angles) / math.sqrt(length)
    imag = -np.sin(angles) / math.sqrt(length)
    forms = []
    for parity in (0, 1):
        c_re, c_im = real[:half, parity::2], imag[:half, parity::2]
        forms.append(np.block([[c_re, c_im], [-c_im, c_re]]))
    forms = np.stack([forms[0], forms[1], forms[0].T, forms[1].T]).astype(np.float32)
    high = forms.astype(ml_dtypes.bfloat16)
    low = (forms - high.astype(np.float32)).astype(ml_dtypes.bfloat16)
    return np.concatenate([high, high, low], axis=1), np.concatenate([high, high, low], axis=2)


def order_matrix(length):
    order = np.concatenate([np.arange(0, length, 2), np.arange(1, length, 2)])
    matrix = np.zeros((length, length), ml_dtypes.bfloat16)
    matrix[order, np.arange(length)] = 1
    return np.stack([matrix, matrix.T])


def parted(value):
    high = value.astype(BF16)
    return high, (value - high.astype(F32)).astype(BF16)


def dot(left, right):
    return jnp.dot(left, right, preferred_element_type=F32)


def on_lanes(value, w, which):
    high, low = parted(value)
    return dot(jnp.concatenate([high, low, high], 1), w[0][which])


def on_rows(value, w, which):
    high, low = parted(value)
    return dot(w[1][which], jnp.concatenate([high, low, high], 0))


def cut(value, axis):
    half = value.shape[axis] // 2
    return (value[:half], value[half:]) if axis == 0 else (value[:, :half], value[:, half:])


def forward(re, im, w):
    for axis, apply, base in ((0, on_rows, 2), (1, on_lanes, 0)):
        re_a, re_b = cut(re, axis)
        im_a, im_b = cut(im, axis)
        even = apply(jnp.concatenate([re_a + re_b, im_a + im_b], axis), w, base)
        odd = apply(jnp.concatenate([re_a - re_b, im_a - im_b], axis), w, base + 1)
        even_re, even_im = cut(even, axis)
        odd_re, odd_im = cut(odd, axis)
        re = jnp.concatenate([even_re, odd_re], axis)
        im = jnp.concatenate([even_im, odd_im], axis)
    return re, im


def backward(re, im, w):
    for axis, apply, base in ((0, on_rows, 0), (1, on_lanes, 2)):
        re_a, re_b = cut(re, axis)
        im_a, im_b = cut(im, axis)
        even = apply(jnp.concatenate([re_a, im_a], axis), w, base)
        odd = apply(jnp.concatenate([re_b, im_b], axis), w, base + 1)
        sum_re, sum_im = cut(even + odd, axis)
        dif_re, dif_im = cut(even - odd, axis)
        re = jnp.concatenate([sum_re, dif_re], axis)
        im = jnp.concatenate([sum_im, dif_im], axis)
    return re, im


def complex_times(left_re, left_im, right_re, right_im):
    return (left_re * right_re - left_im * right_im, left_re * right_im + left_im * right_re)


def conj_times(left_re, left_im, right_re, right_im):
    return (left_re * right_re + left_im * right_im, left_im * right_re - left_re * right_im)


def gather_padded(layer, obj, up, down, left, right, cor_left, cor_right, pad, sem):
    half = up.shape[1]
    tile = obj.shape[-1]
    end = half + tile
    mid, first, last = pl.ds(half, tile), pl.ds(0, half), pl.ds(end, half)
    pairs = [
        (obj.at[layer], pad.at[:, mid, mid]),
        (up, pad.at[:, first, mid]),
        (down, pad.at[:, last, mid]),
        (left.at[layer], pad.at[:, mid, first]),
        (right.at[layer], pad.at[:, mid, last]),
        (cor_left.at[0], pad.at[:, first, first]),
        (cor_left.at[1], pad.at[:, last, first]),
        (cor_right.at[0], pad.at[:, first, last]),
        (cor_right.at[1], pad.at[:, last, last]),
    ]
    copies = [pltpu.make_async_copy(a, b, sem.at[i]) for i, (a, b) in enumerate(pairs)]
    for copy in copies:
        copy.start()
    for copy in copies:
        copy.wait()


def corner(places, slot, patch):
    y, x = places[slot, 0], places[slot, 1]
    row = pl.multiple_of(y // 8 * 8, 8)
    lane = pl.multiple_of(x // 128 * 128, 128)
    return pl.ds(row, patch + 8), pl.ds(lane, patch + 128), y % 8, x % 128


def window(pad, places, slot, patch):
    rows, lanes, down, along = corner(places, slot, patch)
    tall, wide = patch + 8, patch + 128
    found = []
    for c in range(2):
        value = pltpu.roll(pad[c, rows, lanes], (wide - along) % wide, 1)[:, :patch]
        found.append(pltpu.roll(value, (tall - down) % tall, 0)[:patch])
    return found


def add_window(total, places, slot, terms):
    patch = terms[0].shape[0]
    rows, lanes, down, along = corner(places, slot, patch)
    for c in range(2):
        value = jnp.concatenate([terms[c], jnp.zeros((8, patch), F32)], 0)
        value = pltpu.roll(value, down, 0)
        value = jnp.concatenate([value, jnp.zeros((patch + 8, 128), F32)], 1)
        total[c, rows, lanes] += pltpu.roll(value, along, 1)


def write_pieces(total, out_left, out_mid, out_right, out_top, out_bottom):
    half = out_left.shape[-1]
    tile = out_mid.shape[-1]
    rows = out_mid.shape[1]
    out_left[...] = total[:, :rows, :half]
    out_mid[...] = total[:, :rows, half : half + tile]
    out_right[...] = total[:, :rows, half + tile : 2 * half + tile]
    out_top[...] = total[:, :half, 2 * half : tile]
    out_bottom[...] = total[:, half + tile : 2 * half + tile, 2 * half : tile]


def order_kernel(measured, waves, order, out_measured, out_waves):
    def ordered(value):
        for axis in (0, 1):
            high, low = parted(value)
            least = (value - high.astype(F32) - low.astype(F32)).astype(BF16)
            if axis == 0:
                high, low, least = [dot(order[1], part) for part in (high, low, least)]
            else:
                high, low, least = [dot(part, order[0]) for part in (high, low, least)]
            value = high + (low + least)
        return value

    def step(slot, carry):
        out_measured[slot] = ordered(measured[slot])
        return carry

    lax.fori_loop(0, measured.shape[0], step, 0)
    out_waves[0] = ordered(waves[0])
    out_waves[1] = ordered(waves[1])


def first_kernel(
    mine, places, obj, up, down, left, right, cl, cr, probe, prop, w0, w1, phi, pad, sem
):
    w = (w0, w1)
    patch = probe.shape[-1]
    gather_padded(0, obj, up, down, left, right, cl, cr, pad, sem)

    def step(slot, carry):
        o_re, o_im = window(pad, places, slot, patch)
        re, im = complex_times(probe[0], probe[1], o_re, o_im)
        re, im = forward(re, im, w)
        re, im = complex_times(prop[0], prop[1], re, im)
        re, im = backward(re, im, w)
        phi[slot, 0] = re
        phi[slot, 1] = im
        return carry

    lax.fori_loop(0, mine[0], step, 0)


def second_kernel(
    mine, places, obj, up, down, left, right, cl, cr, phi, measured, w0, w1,
    wave, out_left, out_mid, out_right, out_top, out_bottom, pad, total, sem,
):
    w = (w0, w1)
    patch = phi.shape[-1]
    gather_padded(1, obj, up, down, left, right, cl, cr, pad, sem)
    total[...] = jnp.zeros_like(total)

    def step(slot, carry):
        o_re, o_im = window(pad, places, slot, patch)
        re, im = complex_times(phi[slot, 0], phi[slot, 1], o_re, o_im)
        re, im = forward(re, im, w)
        misfit = re * re + im * im - measured[slot]
        re, im = backward(misfit * re, misfit * im, w)
        add_window(total, places, slot, conj_times(re, im, phi[slot, 0], phi[slot, 1]))
        o_re, o_im = window(pad, places, slot, patch)
        re, im = conj_times(re, im, o_re, o_im)
        wave[slot, 0] = re
        wave[slot, 1] = im
        return carry

    lax.fori_loop(0, mine[0], step, 0)
    write_pieces(total, out_left, out_mid, out_right, out_top, out_bottom)


def third_kernel(
    mine, places, wave, probe, prop, w0, w1,
    out_left, out_mid, out_right, out_top, out_bottom, total,
):
    w = (w0, w1)
    total[...] = jnp.zeros_like(total)

    def step(slot, carry):
        re, im = forward(wave[slot, 0], wave[slot, 1], w)
        re, im = conj_times(re, im, prop[0], prop[1])
        re, im = backward(re, im, w)
        add_window(total, places, slot, conj_times(re, im, probe[0], probe[1]))
        return carry

    lax.fori_loop(0, mine[0], step, 0)
    write_pieces(total, out_left, out_mid, out_right, out_top, out_bottom)


def spread(piece, before, after, axis):
    pads = [(0, 0)] * piece.ndim
    pads[axis] = (before, after)
    return jnp.pad(piece, pads)


def shards(object_slices, probe, fresnel_phase, intensity, offsets, counts):
    patch = probe.shape[-1]
    half = patch // 2
    tile = object_slices.shape[-1]
    slots = intensity.shape[2]
    long = tile + 2 * half
    smem = pl.BlockSpec(memory_space=pltpu.SMEM)
    vmem = pl.BlockSpec(memory_space=pltpu.VMEM)
    anym = pl.BlockSpec(memory_space=pl.ANY)
    params = pltpu.CompilerParams(vmem_limit_bytes=48 * 2**20)
    wide_scratch = pltpu.VMEM((2, long + 8, long + 128), F32)
    waves = jax.ShapeDtypeStruct((slots, 2, patch, patch), F32)
    pieces = [
        jax.ShapeDtypeStruct((2, long, half), F32),
        jax.ShapeDtypeStruct((2, long, tile), F32),
        jax.ShapeDtypeStruct((2, long, half), F32),
        jax.ShapeDtypeStruct((2, half, tile - 2 * half), F32),
        jax.ShapeDtypeStruct((2, half, tile - 2 * half), F32),
    ]
    cost = pl.CostEstimate(flops=8 * 10**9, bytes_accessed=10**7, transcendentals=0)

    w0, w1 = [jnp.asarray(form) for form in basis_blocks(patch)]
    first, last = object_slices[:, :, :half], object_slices[:, :, tile - half :]
    up1 = passed_along(last[0], "ty", 1)
    down1 = passed_along(first[0], "ty", -1)
    left = passed_along(object_slices[:, :, :, tile - half :], "tx", 1)
    right = passed_along(object_slices[:, :, :, :half], "tx", -1)
    def corners(up, down):
        ends = jnp.stack([up[:, :, tile - half :], down[:, :, tile - half :]])
        starts = jnp.stack([up[:, :, :half], down[:, :, :half]])
        return passed_along(ends, "tx", 1), passed_along(starts, "tx", -1)

    measured, prop = pl.pallas_call(
        order_kernel,
        out_shape=[
            jax.ShapeDtypeStruct((slots, patch, patch), F32),
            jax.ShapeDtypeStruct((2, patch, patch), F32),
        ],
        in_specs=[vmem] * 3,
        out_specs=[vmem] * 2,
        compiler_params=params,
        cost_estimate=cost,
    )(
        intensity[0, 0],
        jnp.stack([jnp.cos(fresnel_phase), jnp.sin(fresnel_phase)]),
        jnp.asarray(order_matrix(patch)),
    )
    last2, first2, up1, down1, measured, prop = lax.optimization_barrier(
        (last[1], first[1], up1, down1, measured, prop)
    )
    up2 = passed_along(last2, "ty", 1)
    down2 = passed_along(first2, "ty", -1)
    places = offsets[0, 0] + half
    mine = counts[lax.axis_index("ty"), lax.axis_index("tx")].reshape(1)

    phi = pl.pallas_call(
        first_kernel,
        out_shape=waves,
        in_specs=[smem] * 2 + [anym] * 7 + [vmem] * 4,
        out_specs=vmem,
        scratch_shapes=[wide_scratch, pltpu.SemaphoreType.DMA((9,))],
        compiler_params=params,
        cost_estimate=cost,
    )(mine, places, object_slices, up1, down1, left, right, *corners(up1, down1), probe, prop, w0, w1)

    up2, down2, phi = lax.optimization_barrier((up2, down2, phi))
    wave, *pieces2 = pl.pallas_call(
        second_kernel,
        out_shape=[waves] + pieces,
        in_specs=[smem] * 2 + [anym] * 7 + [vmem] * 4,
        out_specs=[vmem] * 6,
        scratch_shapes=[wide_scratch, wide_scratch, pltpu.SemaphoreType.DMA((9,))],
        compiler_params=params,
        cost_estimate=cost,
    )(mine, places, object_slices, up2, down2, left, right, *corners(up2, down2), phi, measured, w0, w1)

    def third(wave):
        return pl.pallas_call(
            third_kernel,
            out_shape=pieces,
            in_specs=[smem] * 2 + [vmem] * 5,
            out_specs=[vmem] * 5,
            scratch_shapes=[wide_scratch],
            compiler_params=params,
            cost_estimate=cost,
        )(mine, places, wave, probe, prop, w0, w1)

    def columns_in(left, right):
        return passed_along(right, "tx", 1), passed_along(left, "tx", -1)

    def rows_in(top, bottom):
        return passed_along(bottom, "ty", 1), passed_along(top, "ty", -1)

    def edges_of(mid, before, after, start):
        rows = slice(start, start + half)
        starts = mid[:, rows, :half] + before[:, rows]
        ends = mid[:, rows, tile - half :] + after[:, rows]
        return jnp.concatenate([starts, ends], axis=2)

    def core(mid, before, after, above, below, edge_above, edge_below):
        whole = mid[:, half : half + tile]
        whole = whole + spread(before[:, half : half + tile], 0, tile - half, 2)
        whole = whole + spread(after[:, half : half + tile], tile - half, 0, 2)

        def joined(middle, edge):
            return jnp.concatenate([edge[:, :, :half], middle, edge[:, :, half:]], axis=2)

        whole = whole + spread(joined(above, edge_above), 0, tile - half, 1)
        return whole + spread(joined(below, edge_below), tile - half, 0, 1)

    left2, mid2, right2, top2, bottom2 = pieces2
    above2, below2 = rows_in(top2, bottom2)
    before2, after2 = columns_in(left2, right2)
    left1, mid1, right1, top1, bottom1 = third(wave)
    above1, below1 = rows_in(top1, bottom1)
    left1, right1, above2, below2 = lax.optimization_barrier((left1, right1, above2, below2))
    before1, after1 = columns_in(left1, right1)

    def both_edges(start):
        return jnp.stack(
            [edges_of(mid1, before1, after1, start), edges_of(mid2, before2, after2, start)]
        )

    tops, bottoms, above1, below1 = lax.optimization_barrier(
        (both_edges(0), both_edges(half + tile), above1, below1)
    )
    edges_above, edges_below = rows_in(tops, bottoms)
    total = jnp.stack(
        [
            core(mid1, before1, after1, above1, below1, edges_above[0], edges_below[0]),
            core(mid2, before2, after2, above2, below2, edges_above[1], edges_below[1]),
        ]
    )
    return object_slices - STEP_SIZE * total


def solution(mesh):
    placed = (
        P(None, None, "ty", "tx"),
        P(),
        P(),
        P("ty", "tx", None, None, None),
        P("ty", "tx", None, None),
        P(),
    )
    return jax.shard_map(
        shards, mesh=mesh, in_specs=placed, out_specs=P(None, None, "ty", "tx"), check_vma=False
    )
```

profile of v0, /device:TPU:17, one launch (start us, length us, event | category | flops | bytes accessed | tf_op | source)
XLA Modules:
  0.0 172.9 jit_solution(1887864503754280213)
XLA Ops:
  0.0 2.8 %slice_bitcast_fusion = (f32[2,128,512]{2,1,0:T(8,128)S(1)}, f32[2,128,512]{2,1,0:T(8,128)S(1)}, f32[2,128,512]{2,1,0:T(8,128)}, f32[2,128,512]{2,1,0:T(8,128)}) fusion(f32[2,2,512,512]{3,2,1,0:T(8,128)} %obj.3), kind=kLoop, calls=%fused_computation.21 | loop fusion | bytes 4194304 | tf_op jit(solution)/shard_map/squeeze | solution.py:282
  2.8 3.0 %collective-permute-start.1 = (f32[2,128,512]{2,1,0:T(8,128)S(1)}, f32[2,128,512]{2,1,0:T(8,128)S(1)}, u32[]{:S(2)}, u32[]{:S(2)}) collective-permute-start(f32[2,128,512]{2,1,0:T(8,128)S(1)} %get-tuple-element.67), channel_id=1, source_target_pairs={{4,0},{8,4},{12,8},{16,12},{20,16},{24,20},{28,24},{5,1},{9,5},{13... | collective-permute-start | bytes 1572872 | tf_op jit(solution)/shard_map/ppermute | solution.py:21
  9.8 3.1 %collective-permute-start.5 = (f32[2,2,512,128]{3,2,1,0:T(8,128)}, f32[2,2,512,128]{3,2,1,0:T(8,128)S(1)}, u32[]{:S(2)}, u32[]{:S(2)}) collective-permute-start(f32[2,2,512,128]{3,2,1,0:T(8,128)} %get-tuple-element.65), channel_id=1, source_target_pairs={{1,0},{2,1},{3,2},{5,4},{6,5},{7,6},{9,8},{10,9},{11,10},{13,12},{... | collective-permute-start | bytes 3145736 | tf_op jit(solution)/shard_map/ppermute | solution.py:21
  13.0 3.0 %collective-permute-start.4 = (f32[2,2,512,128]{3,2,1,0:T(8,128)}, f32[2,2,512,128]{3,2,1,0:T(8,128)S(1)}, u32[]{:S(2)}, u32[]{:S(2)}) collective-permute-start(f32[2,2,512,128]{3,2,1,0:T(8,128)} %get-tuple-element.66), channel_id=1, source_target_pairs={{0,1},{1,2},{2,3},{4,5},{5,6},{6,7},{8,9},{9,10},{10,11},{12,13},{... | collective-permute-start | bytes 3145736 | tf_op jit(solution)/shard_map/ppermute | solution.py:21
  17.0 3.3 %shard_map.91 = (f32[4,256,256]{2,1,0:T(8,128)S(1)}, f32[2,256,256]{2,1,0:T(8,128)S(1)}) custom-call(f32[4,256,256]{2,1,0:T(8,128)S(1)} %bitcast.52, f32[2,256,256]{2,1,0:T(8,128)S(1)} %pad_maximum_fusion.waves, bf16[2,256,256]{2,1,0:T(8,128)(2,1)S(1)} %copy-done.4), custom_call_target="tpu_custom_call" | custom-call | flops 8000000000 | bytes 10000000 | tf_op jit(solution)/shard_map/pallas_call | solution.py:290
  20.4 8.3 %collective-permute-done.1.down = f32[2,128,512]{2,1,0:T(8,128)S(1)} collective-permute-done((f32[2,128,512]{2,1,0:T(8,128)S(1)}, f32[2,128,512]{2,1,0:T(8,128)S(1)}, u32[]{:S(2)}, u32[]{:S(2)}) %collective-permute-start.1) | collective-permute-done | bytes 524320 | tf_op jit(solution)/shard_map/ppermute | solution.py:21
  30.5 3.6 %collective-permute-start.6 = (f32[2,2,128,128]{3,2,1,0:T(8,128)}, f32[2,2,128,128]{3,2,1,0:T(8,128)S(1)}, u32[]{:S(2)}, u32[]{:S(2)}) collective-permute-start(f32[2,2,128,128]{3,2,1,0:T(8,128)} %pad_maximum_fusion.3), channel_id=1, source_target_pairs={{0,1},{1,2},{2,3},{4,5},{5,6},{6,7},{8,9},{9,10},{10,11},{12,13},{... | collective-permute-start | bytes 786440 | tf_op jit(solution)/shard_map/ppermute | solution.py:21
  38.2 4.0 %collective-permute-start.2 = (f32[2,128,512]{2,1,0:T(8,128)}, f32[2,128,512]{2,1,0:T(8,128)S(1)}, u32[]{:S(2)}, u32[]{:S(2)}) collective-permute-start(f32[2,128,512]{2,1,0:T(8,128)} %get-tuple-element.37), channel_id=1, source_target_pairs={{0,4},{4,8},{8,12},{12,16},{16,20},{20,24},{24,28},{1,5},{5,9},{9,... | collective-permute-start | bytes 1572872 | tf_op jit(solution)/shard_map/ppermute | solution.py:21
  46.5 13.0 %shard_map.92.phi = f32[4,2,256,256]{3,2,1,0:T(8,128)} custom-call(s32[1]{0:T(128)} %bitcast.mine, s32[4,2]{1,0:T(4,128)S(1)} %copy.12.places, f32[2,2,512,512]{3,2,1,0:T(8,128)} %obj.3, f32[2,128,512]{2,1,0:T(8,128)S(1)} %collective-permute-done.up, f32[2,128,512]{2,1,0:T(8,128)S(1)} %collective-permute-done.1.down, ...), custom_call_target="tpu_custom_call" | custom-call | flops 8000000000 | bytes 10000000 | tf_op jit(solution)/shard_map/pallas_call | solution.py:313
  59.5 4.8 %collective-permute-done.2.up = f32[2,128,512]{2,1,0:T(8,128)S(1)} collective-permute-done((f32[2,128,512]{2,1,0:T(8,128)}, f32[2,128,512]{2,1,0:T(8,128)S(1)}, u32[]{:S(2)}, u32[]{:S(2)}) %collective-permute-start.2) | collective-permute-done | bytes 524320 | tf_op jit(solution)/shard_map/ppermute | solution.py:21
  65.0 4.4 %collective-permute-start.8 = (f32[2,2,128,128]{3,2,1,0:T(8,128)S(1)}, f32[2,2,128,128]{3,2,1,0:T(8,128)S(1)}, u32[]{:S(2)}, u32[]{:S(2)}) collective-permute-start(f32[2,2,128,128]{3,2,1,0:T(8,128)S(1)} %pad_maximum_fusion.5), channel_id=1, source_target_pairs={{0,1},{1,2},{2,3},{4,5},{5,6},{6,7},{8,9},{9,10},{10,11},{12,13},{... | collective-permute-start | bytes 786440 | tf_op jit(solution)/shard_map/ppermute | solution.py:21
  72.7 4.6 %collective-permute-done.9.cr = f32[2,2,128,128]{3,2,1,0:T(8,128)S(1)} collective-permute-done((f32[2,2,128,128]{3,2,1,0:T(8,128)S(1)}, f32[2,2,128,128]{3,2,1,0:T(8,128)S(1)}, u32[]{:S(2)}, u32[]{:S(2)}) %collective-permute-start.9) | collective-permute-done | bytes 262176 | tf_op jit(solution)/shard_map/ppermute | solution.py:21
  77.3 17.6 %shard_map.93 = (f32[4,2,256,256]{3,2,1,0:T(8,128)}, f32[2,768,128]{2,1,0:T(8,128)S(1)}, f32[2,768,512]{2,1,0:T(8,128)}, f32[2,768,128]{2,1,0:T(8,128)S(1)}, f32...) custom-call(s32[1]{0:T(128)} %bitcast.mine, s32[4,2]{1,0:T(4,128)S(1)} %copy.12.places, f32[2,2,512,512]{3,2,1,0:T(8,128)} %obj.3, ...), custom_call_target="tpu_custom_call" | custom-call | flops 8000000000 | bytes 10000000 | tf_op jit(solution)/shard_map/pallas_call | solution.py:324
  94.9 3.2 %collective-permute-start.10 = (f32[2,128,256]{2,1,0:T(8,128)S(1)}, f32[2,128,256]{2,1,0:T(8,128)S(1)}, u32[]{:S(2)}, u32[]{:S(2)}) collective-permute-start(f32[2,128,256]{2,1,0:T(8,128)S(1)} %get-tuple-element.50), channel_id=1, source_target_pairs={{0,4},{4,8},{8,12},{12,16},{16,20},{20,24},{24,28},{1,5},{5,9},{9,... | collective-permute-start | bytes 786440 | tf_op jit(solution)/shard_map/ppermute | solution.py:21
  98.1 3.0 %collective-permute-start.11 = (f32[2,128,256]{2,1,0:T(8,128)S(1)}, f32[2,128,256]{2,1,0:T(8,128)S(1)}, u32[]{:S(2)}, u32[]{:S(2)}) collective-permute-start(f32[2,128,256]{2,1,0:T(8,128)S(1)} %get-tuple-element.51), channel_id=1, source_target_pairs={{4,0},{8,4},{12,8},{16,12},{20,16},{24,20},{28,24},{5,1},{9,5},{13... | collective-permute-start | bytes 786440 | tf_op jit(solution)/shard_map/ppermute | solution.py:21
  103.0 2.5 %collective-permute-start.15 = (f32[2,768,128]{2,1,0:T(8,128)S(1)}, f32[2,768,128]{2,1,0:T(8,128)S(1)}, u32[]{:S(2)}, u32[]{:S(2)}) collective-permute-start(f32[2,768,128]{2,1,0:T(8,128)S(1)} %get-tuple-element.56), channel_id=1, source_target_pairs={{1,0},{2,1},{3,2},{5,4},{6,5},{7,6},{9,8},{10,9},{11,10},{13,12},{... | collective-permute-start | bytes 2359304 | tf_op jit(solution)/shard_map/ppermute | solution.py:21
  105.5 12.0 %shard_map.94 = (f32[2,768,128]{2,1,0:T(8,128)S(1)}, f32[2,768,512]{2,1,0:T(8,128)}, f32[2,768,128]{2,1,0:T(8,128)S(1)}, f32[2,128,256]{2,1,0:T(8,128)S(1)}, f32[2,128,256]{2,1,0:T(8,128)S(1)}) custom-call(s32[1]{0:T(128)} %bitcast.mine, s32[4,2]{1,0:T(4,128)S(1)} %copy.12.places, f32[4,2,256,256]{3,2,1,0:T(8,128)} %get-tuple-element.46.wave, ...), custom_call_target="tpu_custom_call" | custom-call | flops 8000000000 | bytes 10000000 | tf_op jit(solution)/shard_map/pallas_call | solution.py:335
  124.1 3.9 %collective-permute-start.17 = (f32[2,128,256]{2,1,0:T(8,128)S(1)}, f32[2,128,256]{2,1,0:T(8,128)S(1)}, u32[]{:S(2)}, u32[]{:S(2)}) collective-permute-start(f32[2,128,256]{2,1,0:T(8,128)S(1)} %get-tuple-element.58), channel_id=1, source_target_pairs={{4,0},{8,4},{12,8},{16,12},{20,16},{24,20},{28,24},{5,1},{9,5},{13... | collective-permute-start | bytes 786440 | tf_op jit(solution)/shard_map/ppermute | solution.py:21
  128.3 4.7 %collective-permute-done.13 = f32[2,768,128]{2,1,0:T(8,128)S(1)} collective-permute-done((f32[2,768,128]{2,1,0:T(8,128)S(1)}, f32[2,768,128]{2,1,0:T(8,128)S(1)}, u32[]{:S(2)}, u32[]{:S(2)}) %collective-permute-start.13) | collective-permute-done | bytes 786464 | tf_op jit(solution)/shard_map/ppermute | solution.py:21
  135.7 2.7 %collective-permute-done.17 = f32[2,128,256]{2,1,0:T(8,128)S(1)} collective-permute-done((f32[2,128,256]{2,1,0:T(8,128)S(1)}, f32[2,128,256]{2,1,0:T(8,128)S(1)}, u32[]{:S(2)}, u32[]{:S(2)}) %collective-permute-start.17) | collective-permute-done | bytes 262176 | tf_op jit(solution)/shard_map/ppermute | solution.py:21
  140.4 4.3 %collective-permute-start.19 = (f32[2,2,128,256]{3,2,1,0:T(8,128)S(1)}, f32[2,2,128,256]{3,2,1,0:T(8,128)S(1)}, u32[]{:S(2)}, u32[]{:S(2)}) collective-permute-start(f32[2,2,128,256]{3,2,1,0:T(8,128)S(1)} %pad_maximum_fusion.1), channel_id=1, source_target_pairs={{4,0},{8,4},{12,8},{16,12},{20,16},{24,20},{28,24},{5,1},{9,5},{13... | collective-permute-start | bytes 1572872 | tf_op jit(solution)/shard_map/ppermute | solution.py:21
  144.7 18.1 %collective-permute-done.18 = f32[2,2,128,256]{3,2,1,0:T(8,128)S(1)} collective-permute-done((f32[2,2,128,256]{3,2,1,0:T(8,128)S(1)}, f32[2,2,128,256]{3,2,1,0:T(8,128)S(1)}, u32[]{:S(2)}, u32[]{:S(2)}) %collective-permute-start.18) | collective-permute-done | bytes 524320 | tf_op jit(solution)/shard_map/ppermute | solution.py:21
  162.9 3.4 %collective-permute-done.19 = f32[2,2,128,256]{3,2,1,0:T(8,128)S(1)} collective-permute-done((f32[2,2,128,256]{3,2,1,0:T(8,128)S(1)}, f32[2,2,128,256]{3,2,1,0:T(8,128)S(1)}, u32[]{:S(2)}, u32[]{:S(2)}) %collective-permute-start.19) | collective-permute-done | bytes 524320 | tf_op jit(solution)/shard_map/ppermute | solution.py:21
  169.8 3.0 %fusion = f32[2,2,512,512]{3,2,1,0:T(8,128)} fusion(f32[2,2,512,512]{3,2,1,0:T(8,128)S(1)} %copy-done.10, f32[1,2,512,512]{3,2,1,0:T(8,128)S(1)} %fusion.2, f32[1,2,512,512]{3,2,1,0:T(8,128)S(1)} %fusion.5), kind=kLoop, calls=%fused_computation.1 | loop fusion | flops 3145728 | bytes 12582912 | tf_op jit(solution)/shard_map/sub | solution.py:391
  (97 shorter events, 35.9 us)
Async XLA Ops:
  2.8 25.9 %collective-permute-start.1 = (f32[2,128,512]{2,1,0:T(8,128)S(1)}, f32[2,128,512]{2,1,0:T(8,128)S(1)}, u32[]{:S(2)}, u32[]{:S(2)}) collective-permute-start(f32[2,128,512]{2,1,0:T(8,128)S(1)} %get-tuple-element.67), channel_id=1, source_target_pairs={{4,0},{8,4},{12,8},{16,12},{20,16},{24,20},{28,24},{5,1},{9,5},{13... | collective-permute-start | bytes 1572872 | tf_op jit(solution)/shard_map/ppermute | solution.py:21
  5.9 23.8 %collective-permute-start = (f32[2,128,512]{2,1,0:T(8,128)S(1)}, f32[2,128,512]{2,1,0:T(8,128)S(1)}, u32[]{:S(2)}, u32[]{:S(2)}) collective-permute-start(f32[2,128,512]{2,1,0:T(8,128)S(1)} %get-tuple-element.68), channel_id=1, source_target_pairs={{0,4},{4,8},{8,12},{12,16},{16,20},{20,24},{24,28},{1,5},{5,9},{9,... | collective-permute-start | bytes 1572872 | tf_op jit(solution)/shard_map/ppermute | solution.py:21
  9.8 34.6 %collective-permute-start.5 = (f32[2,2,512,128]{3,2,1,0:T(8,128)}, f32[2,2,512,128]{3,2,1,0:T(8,128)S(1)}, u32[]{:S(2)}, u32[]{:S(2)}) collective-permute-start(f32[2,2,512,128]{3,2,1,0:T(8,128)} %get-tuple-element.65), channel_id=1, source_target_pairs={{1,0},{2,1},{3,2},{5,4},{6,5},{7,6},{9,8},{10,9},{11,10},{13,12},{... | collective-permute-start | bytes 3145736 | tf_op jit(solution)/shard_map/ppermute | solution.py:21
  13.0 31.4 %collective-permute-start.4 = (f32[2,2,512,128]{3,2,1,0:T(8,128)}, f32[2,2,512,128]{3,2,1,0:T(8,128)S(1)}, u32[]{:S(2)}, u32[]{:S(2)}) collective-permute-start(f32[2,2,512,128]{3,2,1,0:T(8,128)} %get-tuple-element.66), channel_id=1, source_target_pairs={{0,1},{1,2},{2,3},{4,5},{5,6},{6,7},{8,9},{9,10},{10,11},{12,13},{... | collective-permute-start | bytes 3145736 | tf_op jit(solution)/shard_map/ppermute | solution.py:21
  30.5 11.7 %collective-permute-start.6 = (f32[2,2,128,128]{3,2,1,0:T(8,128)}, f32[2,2,128,128]{3,2,1,0:T(8,128)S(1)}, u32[]{:S(2)}, u32[]{:S(2)}) collective-permute-start(f32[2,2,128,128]{3,2,1,0:T(8,128)} %pad_maximum_fusion.3), channel_id=1, source_target_pairs={{0,1},{1,2},{2,3},{4,5},{5,6},{6,7},{8,9},{9,10},{10,11},{12,13},{... | collective-permute-start | bytes 786440 | tf_op jit(solution)/shard_map/ppermute | solution.py:21
  34.8 9.6 %collective-permute-start.7 = (f32[2,2,128,128]{3,2,1,0:T(8,128)}, f32[2,2,128,128]{3,2,1,0:T(8,128)}, u32[]{:S(2)}, u32[]{:S(2)}) collective-permute-start(f32[2,2,128,128]{3,2,1,0:T(8,128)} %pad_maximum_fusion.4), channel_id=1, source_target_pairs={{1,0},{2,1},{3,2},{5,4},{6,5},{7,6},{9,8},{10,9},{11,10},{13,12},{... | collective-permute-start | bytes 786440 | tf_op jit(solution)/shard_map/ppermute | solution.py:21
  38.2 26.1 %collective-permute-start.2 = (f32[2,128,512]{2,1,0:T(8,128)}, f32[2,128,512]{2,1,0:T(8,128)S(1)}, u32[]{:S(2)}, u32[]{:S(2)}) collective-permute-start(f32[2,128,512]{2,1,0:T(8,128)} %get-tuple-element.37), channel_id=1, source_target_pairs={{0,4},{4,8},{8,12},{12,16},{16,20},{20,24},{24,28},{1,5},{5,9},{9,... | collective-permute-start | bytes 1572872 | tf_op jit(solution)/shard_map/ppermute | solution.py:21
  42.2 22.7 %collective-permute-start.3 = (f32[2,128,512]{2,1,0:T(8,128)}, f32[2,128,512]{2,1,0:T(8,128)S(1)}, u32[]{:S(2)}, u32[]{:S(2)}) collective-permute-start(f32[2,128,512]{2,1,0:T(8,128)} %get-tuple-element.38), channel_id=1, source_target_pairs={{4,0},{8,4},{12,8},{16,12},{20,16},{24,20},{28,24},{5,1},{9,5},{13... | collective-permute-start | bytes 1572872 | tf_op jit(solution)/shard_map/ppermute | solution.py:21
  65.0 7.7 %collective-permute-start.8 = (f32[2,2,128,128]{3,2,1,0:T(8,128)S(1)}, f32[2,2,128,128]{3,2,1,0:T(8,128)S(1)}, u32[]{:S(2)}, u32[]{:S(2)}) collective-permute-start(f32[2,2,128,128]{3,2,1,0:T(8,128)S(1)} %pad_maximum_fusion.5), channel_id=1, source_target_pairs={{0,1},{1,2},{2,3},{4,5},{5,6},{6,7},{8,9},{9,10},{10,11},{12,13},{... | collective-permute-start | bytes 786440 | tf_op jit(solution)/shard_map/ppermute | solution.py:21
  69.5 36.0 %copy-start.2 = (f32[2,256,256]{2,1,0:T(8,128)S(1)}, f32[2,256,256]{2,1,0:T(8,128)}, u32[]{:S(2)}) copy-start(f32[2,256,256]{2,1,0:T(8,128)} %probe.3) | copy-start | bytes 1572868
  69.5 36.0 %copy-start.3 = (bf16[4,768,256]{2,1,0:T(8,128)(2,1)S(1)}, bf16[4,768,256]{2,1,0:T(8,128)(2,1)}, u32[]{:S(2)}) copy-start(bf16[4,768,256]{2,1,0:T(8,128)(2,1)} %constant.27.clone.w0) | copy-start | bytes 4718596
  69.5 36.0 %copy-start.8 = (f32[2,256,256]{2,1,0:T(8,128)S(1)}, f32[2,256,256]{2,1,0:T(8,128)}, u32[]{:S(2)}) copy-start(f32[2,256,256]{2,1,0:T(8,128)} %copy-done.6) | copy-start | bytes 1572868
  69.5 7.8 %collective-permute-start.9 = (f32[2,2,128,128]{3,2,1,0:T(8,128)S(1)}, f32[2,2,128,128]{3,2,1,0:T(8,128)S(1)}, u32[]{:S(2)}, u32[]{:S(2)}) collective-permute-start(f32[2,2,128,128]{3,2,1,0:T(8,128)S(1)} %pad_maximum_fusion.6), channel_id=1, source_target_pairs={{1,0},{2,1},{3,2},{5,4},{6,5},{7,6},{9,8},{10,9},{11,10},{13,12},{... | collective-permute-start | bytes 786440 | tf_op jit(solution)/shard_map/ppermute | solution.py:21
  94.9 22.6 %collective-permute-start.10 = (f32[2,128,256]{2,1,0:T(8,128)S(1)}, f32[2,128,256]{2,1,0:T(8,128)S(1)}, u32[]{:S(2)}, u32[]{:S(2)}) collective-permute-start(f32[2,128,256]{2,1,0:T(8,128)S(1)} %get-tuple-element.50), channel_id=1, source_target_pairs={{0,4},{4,8},{8,12},{12,16},{16,20},{20,24},{24,28},{1,5},{5,9},{9,... | collective-permute-start | bytes 786440 | tf_op jit(solution)/shard_map/ppermute | solution.py:21
  98.1 19.4 %collective-permute-start.11 = (f32[2,128,256]{2,1,0:T(8,128)S(1)}, f32[2,128,256]{2,1,0:T(8,128)S(1)}, u32[]{:S(2)}, u32[]{:S(2)}) collective-permute-start(f32[2,128,256]{2,1,0:T(8,128)S(1)} %get-tuple-element.51), channel_id=1, source_target_pairs={{4,0},{8,4},{12,8},{16,12},{20,16},{24,20},{28,24},{5,1},{9,5},{13... | collective-permute-start | bytes 786440 | tf_op jit(solution)/shard_map/ppermute | solution.py:21
  101.1 23.0 %collective-permute-start.14 = (f32[2,768,128]{2,1,0:T(8,128)S(1)}, f32[2,768,128]{2,1,0:T(8,128)S(1)}, u32[]{:S(2)}, u32[]{:S(2)}) collective-permute-start(f32[2,768,128]{2,1,0:T(8,128)S(1)} %get-tuple-element.55), channel_id=1, source_target_pairs={{0,1},{1,2},{2,3},{4,5},{5,6},{6,7},{8,9},{9,10},{10,11},{12,13},{... | collective-permute-start | bytes 2359304 | tf_op jit(solution)/shard_map/ppermute | solution.py:21
  103.0 25.1 %collective-permute-start.15 = (f32[2,768,128]{2,1,0:T(8,128)S(1)}, f32[2,768,128]{2,1,0:T(8,128)S(1)}, u32[]{:S(2)}, u32[]{:S(2)}) collective-permute-start(f32[2,768,128]{2,1,0:T(8,128)S(1)} %get-tuple-element.56), channel_id=1, source_target_pairs={{1,0},{2,1},{3,2},{5,4},{6,5},{7,6},{9,8},{10,9},{11,10},{13,12},{... | collective-permute-start | bytes 2359304 | tf_op jit(solution)/shard_map/ppermute | solution.py:21
  105.5 22.6 %copy-start.11 = (f32[2,768,512]{2,1,0:T(8,128)S(1)}, f32[2,768,512]{2,1,0:T(8,128)}, u32[]{:S(2)}) copy-start(f32[2,768,512]{2,1,0:T(8,128)} %get-tuple-element.54) | copy-start | bytes 9437188
  117.5 10.8 %collective-permute-start.12 = (f32[2,768,128]{2,1,0:T(8,128)S(1)}, f32[2,768,128]{2,1,0:T(8,128)S(1)}, u32[]{:S(2)}, u32[]{:S(2)}) collective-permute-start(f32[2,768,128]{2,1,0:T(8,128)S(1)} %get-tuple-element.52), channel_id=1, source_target_pairs={{0,1},{1,2},{2,3},{4,5},{5,6},{6,7},{8,9},{9,10},{10,11},{12,13},{... | collective-permute-start | bytes 2359304 | tf_op jit(solution)/shard_map/ppermute | solution.py:21
  119.4 13.6 %collective-permute-start.13 = (f32[2,768,128]{2,1,0:T(8,128)S(1)}, f32[2,768,128]{2,1,0:T(8,128)S(1)}, u32[]{:S(2)}, u32[]{:S(2)}) collective-permute-start(f32[2,768,128]{2,1,0:T(8,128)S(1)} %get-tuple-element.53), channel_id=1, source_target_pairs={{1,0},{2,1},{3,2},{5,4},{6,5},{7,6},{9,8},{10,9},{11,10},{13,12},{... | collective-permute-start | bytes 2359304 | tf_op jit(solution)/shard_map/ppermute | solution.py:21
  121.9 13.9 %collective-permute-start.16 = (f32[2,128,256]{2,1,0:T(8,128)S(1)}, f32[2,128,256]{2,1,0:T(8,128)S(1)}, u32[]{:S(2)}, u32[]{:S(2)}) collective-permute-start(f32[2,128,256]{2,1,0:T(8,128)S(1)} %get-tuple-element.57), channel_id=1, source_target_pairs={{0,4},{4,8},{8,12},{12,16},{16,20},{20,24},{24,28},{1,5},{5,9},{9,... | collective-permute-start | bytes 786440 | tf_op jit(solution)/shard_map/ppermute | solution.py:21
  124.1 14.3 %collective-permute-start.17 = (f32[2,128,256]{2,1,0:T(8,128)S(1)}, f32[2,128,256]{2,1,0:T(8,128)S(1)}, u32[]{:S(2)}, u32[]{:S(2)}) collective-permute-start(f32[2,128,256]{2,1,0:T(8,128)S(1)} %get-tuple-element.58), channel_id=1, source_target_pairs={{4,0},{8,4},{12,8},{16,12},{20,16},{24,20},{28,24},{5,1},{9,5},{13... | collective-permute-start | bytes 786440 | tf_op jit(solution)/shard_map/ppermute | solution.py:21
  138.4 24.4 %collective-permute-start.18 = (f32[2,2,128,256]{3,2,1,0:T(8,128)S(1)}, f32[2,2,128,256]{3,2,1,0:T(8,128)S(1)}, u32[]{:S(2)}, u32[]{:S(2)}) collective-permute-start(f32[2,2,128,256]{3,2,1,0:T(8,128)S(1)} %pad_maximum_fusion.2), channel_id=1, source_target_pairs={{0,4},{4,8},{8,12},{12,16},{16,20},{20,24},{24,28},{1,5},{5,9},{9,... | collective-permute-start | bytes 1572872 | tf_op jit(solution)/shard_map/ppermute | solution.py:21
  140.4 25.9 %collective-permute-start.19 = (f32[2,2,128,256]{3,2,1,0:T(8,128)S(1)}, f32[2,2,128,256]{3,2,1,0:T(8,128)S(1)}, u32[]{:S(2)}, u32[]{:S(2)}) collective-permute-start(f32[2,2,128,256]{3,2,1,0:T(8,128)S(1)} %pad_maximum_fusion.1), channel_id=1, source_target_pairs={{4,0},{8,4},{12,8},{16,12},{20,16},{24,20},{28,24},{5,1},{9,5},{13... | collective-permute-start | bytes 1572872 | tf_op jit(solution)/shard_map/ppermute | solution.py:21
  (19 other events, 204.7 us)
where the time goes:
time: 174 us; the launch traced here: 173 us
  starting transfers between devices  56.9 us (33%)
  waiting for transfers between devices  50.7 us (29%)
  Pallas kernels  45.9 us (26%)
  local copies, waits for them, and re-layouts  11.8 us (7%)
  other arithmetic  6.95 us (4%)
    ppermute x20, starting transfers between devices, passed_along(): lax.ppermute(value, axis, [(source, source + steps) for source in range(f...  56.9 us
    ppermute x20, waiting for transfers between devices, passed_along(): lax.ppermute(value, axis, [(source, source + steps) for source in range(f...  50.7 us
    pallas_call x1, Pallas kernels, shards(): pl.pallas_call(second_kernel, out_shape=[waves] + pieces, in_specs=[smem]...  17.6 us
    pallas_call x1, Pallas kernels, shards(): pl.pallas_call(first_kernel, out_shape=waves, in_specs=[smem] * 2 + [anym...  13 us
    pallas_call x1, Pallas kernels, third(): pl.pallas_call(third_kernel, out_shape=pieces, in_specs=[smem] * 2 + [vme...  12 us
    unnamed x38, local copies, waits for them, and re-layouts  4 us
  transfers between devices with their start and end apart: 20, of which 12 were waited for; matrix products, arithmetic and copies ran while one was open for 4% of the time, Pallas kernels for 16%

commit v1 on v0

--- a/solution.py
+++ b/solution.py
@@ -103,22 +103,26 @@
     return (left_re * right_re + left_im * right_im, left_im * right_re - left_re * right_im)
 
 
-def gather_padded(layer, obj, up, down, left, right, cor_left, cor_right, pad, sem):
-    half = up.shape[1]
+def gather_padded(layer, obj, rows, left, right, cor_left, cor_right, pad, sem):
+    half = left.shape[-1]
     tile = obj.shape[-1]
     end = half + tile
     mid, first, last = pl.ds(half, tile), pl.ds(0, half), pl.ds(end, half)
     pairs = [
         (obj.at[layer], pad.at[:, mid, mid]),
-        (up, pad.at[:, first, mid]),
-        (down, pad.at[:, last, mid]),
         (left.at[layer], pad.at[:, mid, first]),
         (right.at[layer], pad.at[:, mid, last]),
-        (cor_left.at[0], pad.at[:, first, first]),
-        (cor_left.at[1], pad.at[:, last, first]),
-        (cor_right.at[0], pad.at[:, first, last]),
-        (cor_right.at[1], pad.at[:, last, last]),
     ]
+    for side, there in ((0, first), (1, last)):
+        pairs.append((cor_left.at[layer, side], pad.at[:, there, first]))
+        pairs.append((cor_right.at[layer, side], pad.at[:, there, last]))
+        if len(rows) == 2:
+            pairs.append((rows[side], pad.at[:, there, mid]))
+        else:
+            edge, inner = rows[side], rows[2 + side]
+            pairs.append((edge.at[:, :, pl.ds(0, half)], pad.at[:, there, pl.ds(half, half)]))
+            pairs.append((edge.at[:, :, pl.ds(half, half)], pad.at[:, there, pl.ds(tile, half)]))
+            pairs.append((inner, pad.at[:, there, pl.ds(2 * half, tile - 2 * half)]))
     copies = [pltpu.make_async_copy(a, b, sem.at[i]) for i, (a, b) in enumerate(pairs)]
     for copy in copies:
         copy.start()
@@ -153,15 +157,23 @@
         total[c, rows, lanes] += pltpu.roll(value, along, 1)
 
 
-def write_pieces(total, out_left, out_mid, out_right, out_top, out_bottom):
-    half = out_left.shape[-1]
+def write_pieces(total, out_mid, out_top, out_bottom):
+    half = out_top.shape[1]
     tile = out_mid.shape[-1]
     rows = out_mid.shape[1]
-    out_left[...] = total[:, :rows, :half]
     out_mid[...] = total[:, :rows, half : half + tile]
-    out_right[...] = total[:, :rows, half + tile : 2 * half + tile]
     out_top[...] = total[:, :half, 2 * half : tile]
     out_bottom[...] = total[:, half + tile : 2 * half + tile, 2 * half : tile]
+
+
+def write_sides(total, corners, sides):
+    half = sides[0].shape[-1]
+    tile = sides[0].shape[1]
+    for out_corner, out_side, start in zip(corners, sides, (0, half + tile)):
+        lanes = slice(start, start + half)
+        out_corner[0] = total[:, :half, lanes]
+        out_corner[1] = total[:, half + tile : 2 * half + tile, lanes]
+        out_side[...] = total[:, half : half + tile, lanes]
 
 
 def order_kernel(measured, waves, order, out_measured, out_waves):
@@ -190,7 +202,7 @@
 ):
     w = (w0, w1)
     patch = probe.shape[-1]
-    gather_padded(0, obj, up, down, left, right, cl, cr, pad, sem)
+    gather_padded(0, obj, (up, down), left, right, cl, cr, pad, sem)
 
     def step(slot, carry):
         o_re, o_im = window(pad, places, slot, patch)
@@ -206,12 +218,12 @@
 
 
 def second_kernel(
-    mine, places, obj, up, down, left, right, cl, cr, phi, measured, w0, w1,
-    wave, out_left, out_mid, out_right, out_top, out_bottom, pad, total, sem,
+    mine, places, obj, up, down, up_mid, down_mid, left, right, cl, cr, phi, measured, w0, w1,
+    wave, out_mid, out_top, out_bottom, out_cl, out_cr, out_left, out_right, pad, total, sem,
 ):
     w = (w0, w1)
     patch = phi.shape[-1]
-    gather_padded(1, obj, up, down, left, right, cl, cr, pad, sem)
+    gather_padded(1, obj, (up, down, up_mid, down_mid), left, right, cl, cr, pad, sem)
     total[...] = jnp.zeros_like(total)
 
     def step(slot, carry):
@@ -228,12 +240,13 @@
         return carry
 
     lax.fori_loop(0, mine[0], step, 0)
-    write_pieces(total, out_left, out_mid, out_right, out_top, out_bottom)
+    write_pieces(total, out_mid, out_top, out_bottom)
+    write_sides(total, (out_cl, out_cr), (out_left, out_right))
 
 
 def third_kernel(
-    mine, places, wave, probe, prop, w0, w1,
-    out_left, out_mid, out_right, out_top, out_bottom, total,
+    mine, places, wave, probe, prop, w0, w1, cl, cr, left, right,
+    out_mid, out_top, out_bottom, out_cl, out_cr, out_left, out_right, total,
 ):
     w = (w0, w1)
     total[...] = jnp.zeros_like(total)
@@ -246,7 +259,12 @@
         return carry
 
     lax.fori_loop(0, mine[0], step, 0)
-    write_pieces(total, out_left, out_mid, out_right, out_top, out_bottom)
+    write_pieces(total, out_mid, out_top, out_bottom)
+    write_sides(
+        total, (out_cl.at[0], out_cr.at[0]), (out_left.at[0], out_right.at[0])
+    )
+    for out, value in ((out_cl, cl), (out_cr, cr), (out_left, left), (out_right, right)):
+        out[1] = value[...]
 
 
 def spread(piece, before, after, axis):
@@ -268,25 +286,31 @@
     wide_scratch = pltpu.VMEM((2, long + 8, long + 128), F32)
     waves = jax.ShapeDtypeStruct((slots, 2, patch, patch), F32)
     pieces = [
-        jax.ShapeDtypeStruct((2, long, half), F32),
         jax.ShapeDtypeStruct((2, long, tile), F32),
-        jax.ShapeDtypeStruct((2, long, half), F32),
         jax.ShapeDtypeStruct((2, half, tile - 2 * half), F32),
         jax.ShapeDtypeStruct((2, half, tile - 2 * half), F32),
     ]
+    side_shapes = [(2, 2, half, half)] * 2 + [(2, tile, half)] * 2
+    sides = [jax.ShapeDtypeStruct(shape, F32) for shape in side_shapes]
+    both_sides = [jax.ShapeDtypeStruct((2,) + shape, F32) for shape in side_shapes]
     cost = pl.CostEstimate(flops=8 * 10**9, bytes_accessed=10**7, transcendentals=0)
 
     w0, w1 = [jnp.asarray(form) for form in basis_blocks(patch)]
     first, last = object_slices[:, :, :half], object_slices[:, :, tile - half :]
     up1 = passed_along(last[0], "ty", 1)
     down1 = passed_along(first[0], "ty", -1)
+
+
+    def outer(piece):
+        return jnp.concatenate([piece[:, :, :half], piece[:, :, tile - half :]], axis=2)
+
+    def inner(piece):
+        return piece[:, :, half : tile - half]
+
+    up2 = passed_along(outer(last[1]), "ty", 1)
+    down2 = passed_along(outer(first[1]), "ty", -1)
     left = passed_along(object_slices[:, :, :, tile - half :], "tx", 1)
     right = passed_along(object_slices[:, :, :, :half], "tx", -1)
-    def corners(up, down):
-        ends = jnp.stack([up[:, :, tile - half :], down[:, :, tile - half :]])
-        starts = jnp.stack([up[:, :, :half], down[:, :, :half]])
-        return passed_along(ends, "tx", 1), passed_along(starts, "tx", -1)
-
     measured, prop = pl.pallas_call(
         order_kernel,
         out_shape=[
@@ -303,10 +327,19 @@
         jnp.asarray(order_matrix(patch)),
     )
     last2, first2, up1, down1, measured, prop = lax.optimization_barrier(
-        (last[1], first[1], up1, down1, measured, prop)
-    )
-    up2 = passed_along(last2, "ty", 1)
-    down2 = passed_along(first2, "ty", -1)
+        (inner(last[1]), inner(first[1]), up1, down1, measured, prop)
+    )
+    up2_mid = passed_along(last2, "ty", 1)
+    down2_mid = passed_along(first2, "ty", -1)
+
+    def corners(up, down, up_next, down_next):
+        return jnp.stack([jnp.stack([up, down]), jnp.stack([up_next, down_next])])
+
+    ends = corners(
+        up1[:, :, tile - half :], down1[:, :, tile - half :], up2[:, :, half:], down2[:, :, half:]
+    )
+    starts = corners(up1[:, :, :half], down1[:, :, :half], up2[:, :, :half], down2[:, :, :half])
+    halo = (left, right, passed_along(ends, "tx", 1), passed_along(starts, "tx", -1))
     places = offsets[0, 0] + half
     mine = counts[lax.axis_index("ty"), lax.axis_index("tx")].reshape(1)
 
@@ -315,32 +348,34 @@
         out_shape=waves,
         in_specs=[smem] * 2 + [anym] * 7 + [vmem] * 4,
         out_specs=vmem,
-        scratch_shapes=[wide_scratch, pltpu.SemaphoreType.DMA((9,))],
+        scratch_shapes=[wide_scratch, pltpu.SemaphoreType.DMA((13,))],
         compiler_params=params,
         cost_estimate=cost,
-    )(mine, places, object_slices, up1, down1, left, right, *corners(up1, down1), probe, prop, w0, w1)
-
-    up2, down2, phi = lax.optimization_barrier((up2, down2, phi))
+    )(mine, places, object_slices, up1, down1, *halo, probe, prop, w0, w1)
+
+    up2_mid, down2_mid, phi = lax.optimization_barrier((up2_mid, down2_mid, phi))
     wave, *pieces2 = pl.pallas_call(
         second_kernel,
-        out_shape=[waves] + pieces,
-        in_specs=[smem] * 2 + [anym] * 7 + [vmem] * 4,
-        out_specs=[vmem] * 6,
-        scratch_shapes=[wide_scratch, wide_scratch, pltpu.SemaphoreType.DMA((9,))],
+        out_shape=[waves] + pieces + sides,
+        in_specs=[smem] * 2 + [anym] * 9 + [vmem] * 4,
+        out_specs=[vmem] * 8,
+        scratch_shapes=[wide_scratch, wide_scratch, pltpu.SemaphoreType.DMA((13,))],
         compiler_params=params,
         cost_estimate=cost,
-    )(mine, places, object_slices, up2, down2, left, right, *corners(up2, down2), phi, measured, w0, w1)
-
-    def third(wave):
+    )(
+        mine, places, object_slices, up2, down2, up2_mid, down2_mid, *halo, phi, measured, w0, w1
+    )
+
+    def third(wave, *sides2):
         return pl.pallas_call(
             third_kernel,
-            out_shape=pieces,
-            in_specs=[smem] * 2 + [vmem] * 5,
-            out_specs=[vmem] * 5,
+            out_shape=pieces + both_sides,
+            in_specs=[smem] * 2 + [vmem] * 9,
+            out_specs=[vmem] * 7,
             scratch_shapes=[wide_scratch],
             compiler_params=params,
             cost_estimate=cost,
-        )(mine, places, wave, probe, prop, w0, w1)
+        )(mine, places, wave, probe, prop, w0, w1, *sides2)
 
     def columns_in(left, right):
         return passed_along(right, "tx", 1), passed_along(left, "tx", -1)
@@ -350,14 +385,14 @@
 
     def edges_of(mid, before, after, start):
         rows = slice(start, start + half)
-        starts = mid[:, rows, :half] + before[:, rows]
-        ends = mid[:, rows, tile - half :] + after[:, rows]
+        starts = mid[:, rows, :half] + before
+        ends = mid[:, rows, tile - half :] + after
         return jnp.concatenate([starts, ends], axis=2)
 
     def core(mid, before, after, above, below, edge_above, edge_below):
         whole = mid[:, half : half + tile]
-        whole = whole + spread(before[:, half : half + tile], 0, tile - half, 2)
-        whole = whole + spread(after[:, half : half + tile], tile - half, 0, 2)
+        whole = whole + spread(before, 0, tile - half, 2)
+        whole = whole + spread(after, tile - half, 0, 2)
 
         def joined(middle, edge):
             return jnp.concatenate([edge[:, :, :half], middle, edge[:, :, half:]], axis=2)
@@ -365,27 +400,33 @@
         whole = whole + spread(joined(above, edge_above), 0, tile - half, 1)
         return whole + spread(joined(below, edge_below), tile - half, 0, 1)
 
-    left2, mid2, right2, top2, bottom2 = pieces2
+    mid2, top2, bottom2, *sides2 = pieces2
     above2, below2 = rows_in(top2, bottom2)
-    before2, after2 = columns_in(left2, right2)
-    left1, mid1, right1, top1, bottom1 = third(wave)
+    mid1, top1, bottom1, cor_left, cor_right, side_left, side_right = third(wave, *sides2)
+    cor_left, cor_right, above2, below2 = lax.optimization_barrier(
+        (cor_left, cor_right, above2, below2)
+    )
     above1, below1 = rows_in(top1, bottom1)
-    left1, right1, above2, below2 = lax.optimization_barrier((left1, right1, above2, below2))
-    before1, after1 = columns_in(left1, right1)
-
-    def both_edges(start):
+    cor_before, cor_after = columns_in(cor_left, cor_right)
+
+    def both_edges(side):
+        start = side * (half + tile)
         return jnp.stack(
-            [edges_of(mid1, before1, after1, start), edges_of(mid2, before2, after2, start)]
+            [
+                edges_of(mid1, cor_before[0, side], cor_after[0, side], start),
+                edges_of(mid2, cor_before[1, side], cor_after[1, side], start),
+            ]
         )
 
-    tops, bottoms, above1, below1 = lax.optimization_barrier(
-        (both_edges(0), both_edges(half + tile), above1, below1)
+    tops, bottoms, above1, below1, side_left, side_right = lax.optimization_barrier(
+        (both_edges(0), both_edges(1), above1, below1, side_left, side_right)
     )
     edges_above, edges_below = rows_in(tops, bottoms)
+    before, after = columns_in(side_left, side_right)
     total = jnp.stack(
         [
-            core(mid1, before1, after1, above1, below1, edges_above[0], edges_below[0]),
-            core(mid2, before2, after2, above2, below2, edges_above[1], edges_below[1]),
+            core(mid1, before[0], after[0], above1, below1, edges_above[0], edges_below[0]),
+            core(mid2, before[1], after[1], above2, below2, edges_above[1], edges_below[1]),
         ]
     )
     return object_slices - STEP_SIZE * total

time: 174 us -> 166 us (0.954); the launches traced: 173 us -> 163 us
  starting transfers between devices: 56.9 us -> 77.2 us
  waiting for transfers between devices: 50.7 us -> 31.1 us
  Pallas kernels: 45.9 us -> 35.4 us
    ppermute x20, starting transfers between devices: 56.9 us -> 77.2 us  [passed_along(): lax.ppermute(value, axis, [(source, source + steps) for source in range(f...]
    ppermute x20, waiting for transfers between devices: 50.7 us -> 31.1 us  [passed_along(): lax.ppermute(value, axis, [(source, source + steps) for source in range(f...]
    pallas_call x2, Pallas kernels: 29.5 us -> 22.6 us  [the longest x1 13.1 us: shards(): pl.pallas_call(second_kernel, out_shape=[waves] + pieces + sides, in_spec...]
    pallas_call x1, Pallas kernels: 13 us -> 9.4 us  [shards(): pl.pallas_call(first_kernel, out_shape=waves, in_specs=[smem] * 2 + [anym...]
    unnamed x38 -> x30, local copies, waits for them, and re-layouts: 4 us -> 4.83 us
  transfers between devices with their start and end apart: 20 -> 20, of which waited for: 12 -> 7; matrix products, arithmetic and copies ran while one was open for 4% -> 5% of each run, Pallas kernels for 16% -> 14%
where the time goes in v1:
time: 166 us; the launch traced here: 163 us
  starting transfers between devices  77.2 us (47%)
  Pallas kernels  35.4 us (21%)
  waiting for transfers between devices  31.1 us (19%)
  local copies, waits for them, and re-layouts  11.7 us (7%)
  other arithmetic  6.96 us (4%)
    ppermute x20, starting transfers between devices, passed_along(): lax.ppermute(value, axis, [(source, source + steps) for source in range(f...  77.2 us
    ppermute x20, waiting for transfers between devices, passed_along(): lax.ppermute(value, axis, [(source, source + steps) for source in range(f...  31.1 us
    pallas_call x1, Pallas kernels, shards(): pl.pallas_call(second_kernel, out_shape=[waves] + pieces + sides, in_spec...  13.1 us
    pallas_call x1, Pallas kernels, third(): pl.pallas_call(third_kernel, out_shape=pieces + both_sides, in_specs=[sme...  9.47 us
    pallas_call x1, Pallas kernels, shards(): pl.pallas_call(first_kernel, out_shape=waves, in_specs=[smem] * 2 + [anym...  9.4 us
    unnamed x30, local copies, waits for them, and re-layouts  4.83 us
    pallas_call x1, Pallas kernels, shards(): pl.pallas_call(order_kernel, out_shape=[jax.ShapeDtypeStruct((slots, patc...  3.35 us
  transfers between devices with their start and end apart: 20, of which 7 were waited for; matrix products, arithmetic and copies ran while one was open for 5% of the time, Pallas kernels for 14%

profile of v1, /device:TPU:17, one launch (start us, length us, event | category | flops | bytes accessed | tf_op | source)
XLA Modules:
  0.0 163.0 jit_solution(2548341487986678616)
XLA Ops:
  1.9 3.1 %collective-permute-start = (f32[2,128,256]{2,1,0:T(8,128)S(1)}, f32[2,128,256]{2,1,0:T(8,128)S(1)}, u32[]{:S(2)}, u32[]{:S(2)}) collective-permute-start(f32[2,128,256]{2,1,0:T(8,128)S(1)} %pad_maximum_fusion.5), channel_id=1, source_target_pairs={{0,4},{4,8},{8,12},{12,16},{16,20},{20,24},{24,28},{1,5},{5,9},{9,... | collective-permute-start | bytes 786440 | tf_op jit(solution)/shard_map/ppermute | solution.py:21
  5.1 3.0 %collective-permute-start.1 = (f32[2,128,256]{2,1,0:T(8,128)S(1)}, f32[2,128,256]{2,1,0:T(8,128)S(1)}, u32[]{:S(2)}, u32[]{:S(2)}) collective-permute-start(f32[2,128,256]{2,1,0:T(8,128)S(1)} %pad_maximum_fusion.6), channel_id=1, source_target_pairs={{4,0},{8,4},{12,8},{16,12},{20,16},{24,20},{28,24},{5,1},{9,5},{13... | collective-permute-start | bytes 786440 | tf_op jit(solution)/shard_map/ppermute | solution.py:21
  8.1 2.1 %collective-permute-start.3 = (f32[2,128,512]{2,1,0:T(8,128)S(1)}, f32[2,128,512]{2,1,0:T(8,128)S(1)}, u32[]{:S(2)}, u32[]{:S(2)}) collective-permute-start(f32[2,128,512]{2,1,0:T(8,128)S(1)} %get-tuple-element.79), channel_id=1, source_target_pairs={{4,0},{8,4},{12,8},{16,12},{20,16},{24,20},{28,24},{5,1},{9,5},{13... | collective-permute-start | bytes 1572872 | tf_op jit(solution)/shard_map/ppermute | solution.py:21
  10.3 3.3 %collective-permute-start.2 = (f32[2,128,512]{2,1,0:T(8,128)S(1)}, f32[2,128,512]{2,1,0:T(8,128)S(1)}, u32[]{:S(2)}, u32[]{:S(2)}) collective-permute-start(f32[2,128,512]{2,1,0:T(8,128)S(1)} %get-tuple-element.80), channel_id=1, source_target_pairs={{0,4},{4,8},{8,12},{12,16},{16,20},{20,24},{24,28},{1,5},{5,9},{9,... | collective-permute-start | bytes 1572872 | tf_op jit(solution)/shard_map/ppermute | solution.py:21
  15.1 3.7 %collective-permute-start.7 = (f32[2,2,512,128]{3,2,1,0:T(8,128)}, f32[2,2,512,128]{3,2,1,0:T(8,128)S(1)}, u32[]{:S(2)}, u32[]{:S(2)}) collective-permute-start(f32[2,2,512,128]{3,2,1,0:T(8,128)} %get-tuple-element.77), channel_id=1, source_target_pairs={{1,0},{2,1},{3,2},{5,4},{6,5},{7,6},{9,8},{10,9},{11,10},{13,12},{... | collective-permute-start | bytes 3145736 | tf_op jit(solution)/shard_map/ppermute | solution.py:21
  19.9 3.3 %shard_map.91 = (f32[4,256,256]{2,1,0:T(8,128)S(1)}, f32[2,256,256]{2,1,0:T(8,128)S(1)}) custom-call(f32[4,256,256]{2,1,0:T(8,128)S(1)} %bitcast.100, f32[2,256,256]{2,1,0:T(8,128)S(1)} %pad_maximum_fusion.waves, bf16[2,256,256]{2,1,0:T(8,128)(2,1)S(1)} %copy-done.3), custom_call_target="tpu_custom_call" | custom-call | flops 8000000000 | bytes 10000000 | tf_op jit(solution)/shard_map/pallas_call | solution.py:314
  24.1 8.5 %collective-permute-start.6 = (f32[2,2,512,128]{3,2,1,0:T(8,128)}, f32[2,2,512,128]{3,2,1,0:T(8,128)}, u32[]{:S(2)}, u32[]{:S(2)}) collective-permute-start(f32[2,2,512,128]{3,2,1,0:T(8,128)} %get-tuple-element.78), channel_id=1, source_target_pairs={{0,1},{1,2},{2,3},{4,5},{5,6},{6,7},{8,9},{9,10},{10,11},{12,13},{... | collective-permute-start | bytes 3145736 | tf_op jit(solution)/shard_map/ppermute | solution.py:21
  32.7 8.3 %collective-permute-done.3.down = f32[2,128,512]{2,1,0:T(8,128)S(1)} collective-permute-done((f32[2,128,512]{2,1,0:T(8,128)S(1)}, f32[2,128,512]{2,1,0:T(8,128)S(1)}, u32[]{:S(2)}, u32[]{:S(2)}) %collective-permute-start.3) | collective-permute-done | bytes 524320 | tf_op jit(solution)/shard_map/ppermute | solution.py:21
  42.0 3.5 %collective-permute-start.8 = (f32[2,2,2,128,128]{4,3,2,1,0:T(8,128)}, f32[2,2,2,128,128]{4,3,2,1,0:T(8,128)}, u32[]{:S(2)}, u32[]{:S(2)}) collective-permute-start(f32[2,2,2,128,128]{4,3,2,1,0:T(8,128)} %pad_maximum_fusion.1), channel_id=1, source_target_pairs={{0,1},{1,2},{2,3},{4,5},{5,6},{6,7},{8,9},{9,10},{10,11},{12,13},{... | collective-permute-start | bytes 1572872 | tf_op jit(solution)/shard_map/ppermute | solution.py:21
  49.7 2.2 %collective-permute-start.4 = (f32[2,128,256]{2,1,0:T(8,128)}, f32[2,128,256]{2,1,0:T(8,128)S(1)}, u32[]{:S(2)}, u32[]{:S(2)}) collective-permute-start(f32[2,128,256]{2,1,0:T(8,128)} %slice.228), channel_id=1, source_target_pairs={{0,4},{4,8},{8,12},{12,16},{16,20},{20,24},{24,28},{1,5},{5,9},{9,... | collective-permute-start | bytes 786440 | tf_op jit(solution)/shard_map/ppermute | solution.py:21
  51.9 3.9 %collective-permute-start.5 = (f32[2,128,256]{2,1,0:T(8,128)S(1)}, f32[2,128,256]{2,1,0:T(8,128)S(1)}, u32[]{:S(2)}, u32[]{:S(2)}) collective-permute-start(f32[2,128,256]{2,1,0:T(8,128)S(1)} %slice.229), channel_id=1, source_target_pairs={{4,0},{8,4},{12,8},{16,12},{20,16},{24,20},{28,24},{5,1},{9,5},{13... | collective-permute-start | bytes 786440 | tf_op jit(solution)/shard_map/ppermute | solution.py:21
  58.8 9.4 %shard_map.92.phi = f32[4,2,256,256]{3,2,1,0:T(8,128)} custom-call(s32[1]{0:T(128)} %bitcast.mine, s32[4,2]{1,0:T(4,128)S(1)} %copy.12.places, f32[2,2,512,512]{3,2,1,0:T(8,128)} %obj.3, f32[2,128,512]{2,1,0:T(8,128)S(1)} %collective-permute-done.2.up, f32[2,128,512]{2,1,0:T(8,128)S(1)} %collective-permute-done.3.down, ...), custom_call_target="tpu_custom_call" | custom-call | flops 8000000000 | bytes 10000000 | tf_op jit(solution)/shard_map/pallas_call | solution.py:346
  68.2 13.1 %shard_map.93 = (f32[4,2,256,256]{3,2,1,0:T(8,128)}, f32[2,768,512]{2,1,0:T(8,128)}, f32[2,128,256]{2,1,0:T(8,128)S(1)}, f32[2,128,256]{2,1,0:T(8,128)S(1)}, f32...) custom-call(s32[1]{0:T(128)} %bitcast.mine, ...), custom_call_target="tpu_custom_call" | custom-call | flops 8000000000 | bytes 10000000 | tf_op jit(solution)/shard_map/pallas_call | solution.py:357
  83.3 10.6 %collective-permute-start.11 = (f32[2,128,256]{2,1,0:T(8,128)S(1)}, f32[2,128,256]{2,1,0:T(8,128)S(1)}, u32[]{:S(2)}, u32[]{:S(2)}) collective-permute-start(f32[2,128,256]{2,1,0:T(8,128)S(1)} %get-tuple-element.61), channel_id=1, source_target_pairs={{4,0},{8,4},{12,8},{16,12},{20,16},{24,20},{28,24},{5,1},{9,5},{13... | collective-permute-start | bytes 786440 | tf_op jit(solution)/shard_map/ppermute | solution.py:21
  93.9 9.5 %shard_map.94 = (f32[2,768,512]{2,1,0:T(8,128)}, f32[2,128,256]{2,1,0:T(8,128)S(1)}, f32[2,128,256]{2,1,0:T(8,128)S(1)}, f32[2,2,2,128,128]{4,3,2,1,0:T(8,128)S(...) custom-call(s32[1]{0:T(128)} %bitcast.mine, ...), custom_call_target="tpu_custom_call" | custom-call | flops 8000000000 | bytes 10000000 | tf_op jit(solution)/shard_map/pallas_call | solution.py:370
  105.3 2.4 %collective-permute-start.13 = (f32[2,2,2,128,128]{4,3,2,1,0:T(8,128)S(1)}, f32[2,2,2,128,128]{4,3,2,1,0:T(8,128)S(1)}, u32[]{:S(2)}, u32[]{:S(2)}) collective-permute-start(f32[2,2,2,128,128]{4,3,2,1,0:T(8,128)S(1)} %get-tuple-element.63), channel_id=1, source_target_pairs={{1,0},{2,1},{3,2},{5,4},{6,5},{7,6},{9,8},{10,9},{11,10},{13,12},{... | collective-permute-start | bytes 1572872 | tf_op jit(solution)/shard_map/ppermute | solution.py:21
  109.7 6.7 %collective-permute-start.15 = (f32[2,128,256]{2,1,0:T(8,128)S(1)}, f32[2,128,256]{2,1,0:T(8,128)S(1)}, u32[]{:S(2)}, u32[]{:S(2)}) collective-permute-start(f32[2,128,256]{2,1,0:T(8,128)S(1)} %get-tuple-element.66), channel_id=1, source_target_pairs={{4,0},{8,4},{12,8},{16,12},{20,16},{24,20},{28,24},{5,1},{9,5},{13... | collective-permute-start | bytes 786440 | tf_op jit(solution)/shard_map/ppermute | solution.py:21
  117.9 2.8 %collective-permute-done.14 = f32[2,128,256]{2,1,0:T(8,128)S(1)} collective-permute-done((f32[2,128,256]{2,1,0:T(8,128)S(1)}, f32[2,128,256]{2,1,0:T(8,128)S(1)}, u32[]{:S(2)}, u32[]{:S(2)}) %collective-permute-start.14) | collective-permute-done | bytes 262176 | tf_op jit(solution)/shard_map/ppermute | solution.py:21
  120.7 4.5 %collective-permute-done.15 = f32[2,128,256]{2,1,0:T(8,128)S(1)} collective-permute-done((f32[2,128,256]{2,1,0:T(8,128)S(1)}, f32[2,128,256]{2,1,0:T(8,128)S(1)}, u32[]{:S(2)}, u32[]{:S(2)}) %collective-permute-start.15) | collective-permute-done | bytes 262176 | tf_op jit(solution)/shard_map/ppermute | solution.py:21
  127.1 5.7 %collective-permute-start.19 = (f32[2,2,128,256]{3,2,1,0:T(8,128)S(1)}, f32[2,2,128,256]{3,2,1,0:T(8,128)S(1)}, u32[]{:S(2)}, u32[]{:S(2)}) collective-permute-start(f32[2,2,128,256]{3,2,1,0:T(8,128)S(1)} %pad_maximum_fusion.3), channel_id=1, source_target_pairs={{4,0},{8,4},{12,8},{16,12},{20,16},{24,20},{28,24},{5,1},{9,5},{13... | collective-permute-start | bytes 1572872 | tf_op jit(solution)/shard_map/ppermute | solution.py:21
  132.8 6.8 %collective-permute-start.16 = (f32[2,2,512,128]{3,2,1,0:T(8,128)S(1)}, f32[2,2,512,128]{3,2,1,0:T(8,128)S(1)}, u32[]{:S(2)}, u32[]{:S(2)}) collective-permute-start(f32[2,2,512,128]{3,2,1,0:T(8,128)S(1)} %copy-done.14), channel_id=1, source_target_pairs={{0,1},{1,2},{2,3},{4,5},{5,6},{6,7},{8,9},{9,10},{10,11},{12,13},{... | collective-permute-start | bytes 3145736 | tf_op jit(solution)/shard_map/ppermute | solution.py:21
  141.6 8.0 %collective-permute-done.18 = f32[2,2,128,256]{3,2,1,0:T(8,128)S(1)} collective-permute-done((f32[2,2,128,256]{3,2,1,0:T(8,128)S(1)}, f32[2,2,128,256]{3,2,1,0:T(8,128)S(1)}, u32[]{:S(2)}, u32[]{:S(2)}) %collective-permute-start.18) | collective-permute-done | bytes 524320 | tf_op jit(solution)/shard_map/ppermute | solution.py:21
  149.7 4.1 %collective-permute-done.19 = f32[2,2,128,256]{3,2,1,0:T(8,128)S(1)} collective-permute-done((f32[2,2,128,256]{3,2,1,0:T(8,128)S(1)}, f32[2,2,128,256]{3,2,1,0:T(8,128)S(1)}, u32[]{:S(2)}, u32[]{:S(2)}) %collective-permute-start.19) | collective-permute-done | bytes 524320 | tf_op jit(solution)/shard_map/ppermute | solution.py:21
  159.9 3.0 %fusion = f32[2,2,512,512]{3,2,1,0:T(8,128)} fusion(f32[2,2,512,512]{3,2,1,0:T(8,128)S(1)} %copy-done.9, f32[1,2,512,512]{3,2,1,0:T(8,128)S(1)} %fusion.2, f32[1,2,512,512]{3,2,1,0:T(8,128)S(1)} %fusion.5), kind=kLoop, calls=%fused_computation.1 | loop fusion | flops 3145728 | bytes 12582912 | tf_op jit(solution)/shard_map/sub | solution.py:432
  (89 shorter events, 30.5 us)
Async XLA Ops:
  1.9 22.2 %collective-permute-start = (f32[2,128,256]{2,1,0:T(8,128)S(1)}, f32[2,128,256]{2,1,0:T(8,128)S(1)}, u32[]{:S(2)}, u32[]{:S(2)}) collective-permute-start(f32[2,128,256]{2,1,0:T(8,128)S(1)} %pad_maximum_fusion.5), channel_id=1, source_target_pairs={{0,4},{4,8},{8,12},{12,16},{16,20},{20,24},{24,28},{1,5},{5,9},{9,... | collective-permute-start | bytes 786440 | tf_op jit(solution)/shard_map/ppermute | solution.py:21
  5.1 27.5 %collective-permute-start.1 = (f32[2,128,256]{2,1,0:T(8,128)S(1)}, f32[2,128,256]{2,1,0:T(8,128)S(1)}, u32[]{:S(2)}, u32[]{:S(2)}) collective-permute-start(f32[2,128,256]{2,1,0:T(8,128)S(1)} %pad_maximum_fusion.6), channel_id=1, source_target_pairs={{4,0},{8,4},{12,8},{16,12},{20,16},{24,20},{28,24},{5,1},{9,5},{13... | collective-permute-start | bytes 786440 | tf_op jit(solution)/shard_map/ppermute | solution.py:21
  8.1 32.9 %collective-permute-start.3 = (f32[2,128,512]{2,1,0:T(8,128)S(1)}, f32[2,128,512]{2,1,0:T(8,128)S(1)}, u32[]{:S(2)}, u32[]{:S(2)}) collective-permute-start(f32[2,128,512]{2,1,0:T(8,128)S(1)} %get-tuple-element.79), channel_id=1, source_target_pairs={{4,0},{8,4},{12,8},{16,12},{20,16},{24,20},{28,24},{5,1},{9,5},{13... | collective-permute-start | bytes 1572872 | tf_op jit(solution)/shard_map/ppermute | solution.py:21
  10.3 30.7 %collective-permute-start.2 = (f32[2,128,512]{2,1,0:T(8,128)S(1)}, f32[2,128,512]{2,1,0:T(8,128)S(1)}, u32[]{:S(2)}, u32[]{:S(2)}) collective-permute-start(f32[2,128,512]{2,1,0:T(8,128)S(1)} %get-tuple-element.80), channel_id=1, source_target_pairs={{0,4},{4,8},{8,12},{12,16},{16,20},{20,24},{24,28},{1,5},{5,9},{9,... | collective-permute-start | bytes 1572872 | tf_op jit(solution)/shard_map/ppermute | solution.py:21
  15.1 42.2 %collective-permute-start.7 = (f32[2,2,512,128]{3,2,1,0:T(8,128)}, f32[2,2,512,128]{3,2,1,0:T(8,128)S(1)}, u32[]{:S(2)}, u32[]{:S(2)}) collective-permute-start(f32[2,2,512,128]{3,2,1,0:T(8,128)} %get-tuple-element.77), channel_id=1, source_target_pairs={{1,0},{2,1},{3,2},{5,4},{6,5},{7,6},{9,8},{10,9},{11,10},{13,12},{... | collective-permute-start | bytes 3145736 | tf_op jit(solution)/shard_map/ppermute | solution.py:21
  23.2 17.9 %copy-start.4 = (f32[4,256,256]{2,1,0:T(8,128)}, f32[4,256,256]{2,1,0:T(8,128)S(1)}, u32[]{:S(2)}) copy-start(f32[4,256,256]{2,1,0:T(8,128)S(1)} %get-tuple-element.51.measured) | copy-start | bytes 3145732
  23.2 17.9 %copy-start.5 = (f32[2,256,256]{2,1,0:T(8,128)}, f32[2,256,256]{2,1,0:T(8,128)S(1)}, u32[]{:S(2)}) copy-start(f32[2,256,256]{2,1,0:T(8,128)S(1)} %get-tuple-element.47.prop) | copy-start | bytes 1572868
  24.1 33.2 %collective-permute-start.6 = (f32[2,2,512,128]{3,2,1,0:T(8,128)}, f32[2,2,512,128]{3,2,1,0:T(8,128)}, u32[]{:S(2)}, u32[]{:S(2)}) collective-permute-start(f32[2,2,512,128]{3,2,1,0:T(8,128)} %get-tuple-element.78), channel_id=1, source_target_pairs={{0,1},{1,2},{2,3},{4,5},{5,6},{6,7},{8,9},{9,10},{10,11},{12,13},{... | collective-permute-start | bytes 3145736 | tf_op jit(solution)/shard_map/ppermute | solution.py:21
  42.0 9.9 %collective-permute-start.8 = (f32[2,2,2,128,128]{4,3,2,1,0:T(8,128)}, f32[2,2,2,128,128]{4,3,2,1,0:T(8,128)}, u32[]{:S(2)}, u32[]{:S(2)}) collective-permute-start(f32[2,2,2,128,128]{4,3,2,1,0:T(8,128)} %pad_maximum_fusion.1), channel_id=1, source_target_pairs={{0,1},{1,2},{2,3},{4,5},{5,6},{6,7},{8,9},{9,10},{10,11},{12,13},{... | collective-permute-start | bytes 1572872 | tf_op jit(solution)/shard_map/ppermute | solution.py:21
  46.3 11.0 %collective-permute-start.9 = (f32[2,2,2,128,128]{4,3,2,1,0:T(8,128)}, f32[2,2,2,128,128]{4,3,2,1,0:T(8,128)}, u32[]{:S(2)}, u32[]{:S(2)}) collective-permute-start(f32[2,2,2,128,128]{4,3,2,1,0:T(8,128)} %pad_maximum_fusion.2), channel_id=1, source_target_pairs={{1,0},{2,1},{3,2},{5,4},{6,5},{7,6},{9,8},{10,9},{11,10},{13,12},{... | collective-permute-start | bytes 1572872 | tf_op jit(solution)/shard_map/ppermute | solution.py:21
  49.7 18.5 %collective-permute-start.4 = (f32[2,128,256]{2,1,0:T(8,128)}, f32[2,128,256]{2,1,0:T(8,128)S(1)}, u32[]{:S(2)}, u32[]{:S(2)}) collective-permute-start(f32[2,128,256]{2,1,0:T(8,128)} %slice.228), channel_id=1, source_target_pairs={{0,4},{4,8},{8,12},{12,16},{16,20},{20,24},{24,28},{1,5},{5,9},{9,... | collective-permute-start | bytes 786440 | tf_op jit(solution)/shard_map/ppermute | solution.py:21
  51.9 16.3 %collective-permute-start.5 = (f32[2,128,256]{2,1,0:T(8,128)S(1)}, f32[2,128,256]{2,1,0:T(8,128)S(1)}, u32[]{:S(2)}, u32[]{:S(2)}) collective-permute-start(f32[2,128,256]{2,1,0:T(8,128)S(1)} %slice.229), channel_id=1, source_target_pairs={{4,0},{8,4},{12,8},{16,12},{20,16},{24,20},{28,24},{5,1},{9,5},{13... | collective-permute-start | bytes 786440 | tf_op jit(solution)/shard_map/ppermute | solution.py:21
  68.2 25.7 %copy-start.7 = (f32[2,256,256]{2,1,0:T(8,128)S(1)}, f32[2,256,256]{2,1,0:T(8,128)}, u32[]{:S(2)}) copy-start(f32[2,256,256]{2,1,0:T(8,128)} %copy-done.5) | copy-start | bytes 1572868
  81.4 22.0 %collective-permute-start.10 = (f32[2,128,256]{2,1,0:T(8,128)S(1)}, f32[2,128,256]{2,1,0:T(8,128)S(1)}, u32[]{:S(2)}, u32[]{:S(2)}) collective-permute-start(f32[2,128,256]{2,1,0:T(8,128)S(1)} %get-tuple-element.60), channel_id=1, source_target_pairs={{0,4},{4,8},{8,12},{12,16},{16,20},{20,24},{24,28},{1,5},{5,9},{9,... | collective-permute-start | bytes 786440 | tf_op jit(solution)/shard_map/ppermute | solution.py:21
  83.3 20.1 %collective-permute-start.11 = (f32[2,128,256]{2,1,0:T(8,128)S(1)}, f32[2,128,256]{2,1,0:T(8,128)S(1)}, u32[]{:S(2)}, u32[]{:S(2)}) collective-permute-start(f32[2,128,256]{2,1,0:T(8,128)S(1)} %get-tuple-element.61), channel_id=1, source_target_pairs={{4,0},{8,4},{12,8},{16,12},{20,16},{24,20},{28,24},{5,1},{9,5},{13... | collective-permute-start | bytes 786440 | tf_op jit(solution)/shard_map/ppermute | solution.py:21
  93.9 22.5 %copy-start.10 = (f32[2,768,512]{2,1,0:T(8,128)S(1)}, f32[2,768,512]{2,1,0:T(8,128)}, u32[]{:S(2)}) copy-start(f32[2,768,512]{2,1,0:T(8,128)} %get-tuple-element.64) | copy-start | bytes 9437188
  103.4 13.0 %collective-permute-start.12 = (f32[2,2,2,128,128]{4,3,2,1,0:T(8,128)S(1)}, f32[2,2,2,128,128]{4,3,2,1,0:T(8,128)S(1)}, u32[]{:S(2)}, u32[]{:S(2)}) collective-permute-start(f32[2,2,2,128,128]{4,3,2,1,0:T(8,128)S(1)} %get-tuple-element.62), channel_id=1, source_target_pairs={{0,1},{1,2},{2,3},{4,5},{5,6},{6,7},{8,9},{9,10},{10,11},{12,13},{... | collective-permute-start | bytes 1572872 | tf_op jit(solution)/shard_map/ppermute | solution.py:21
  105.3 11.1 %collective-permute-start.13 = (f32[2,2,2,128,128]{4,3,2,1,0:T(8,128)S(1)}, f32[2,2,2,128,128]{4,3,2,1,0:T(8,128)S(1)}, u32[]{:S(2)}, u32[]{:S(2)}) collective-permute-start(f32[2,2,2,128,128]{4,3,2,1,0:T(8,128)S(1)} %get-tuple-element.63), channel_id=1, source_target_pairs={{1,0},{2,1},{3,2},{5,4},{6,5},{7,6},{9,8},{10,9},{11,10},{13,12},{... | collective-permute-start | bytes 1572872 | tf_op jit(solution)/shard_map/ppermute | solution.py:21
  107.8 12.9 %collective-permute-start.14 = (f32[2,128,256]{2,1,0:T(8,128)S(1)}, f32[2,128,256]{2,1,0:T(8,128)S(1)}, u32[]{:S(2)}, u32[]{:S(2)}) collective-permute-start(f32[2,128,256]{2,1,0:T(8,128)S(1)} %get-tuple-element.65), channel_id=1, source_target_pairs={{0,4},{4,8},{8,12},{12,16},{16,20},{20,24},{24,28},{1,5},{5,9},{9,... | collective-permute-start | bytes 786440 | tf_op jit(solution)/shard_map/ppermute | solution.py:21
  109.7 15.5 %collective-permute-start.15 = (f32[2,128,256]{2,1,0:T(8,128)S(1)}, f32[2,128,256]{2,1,0:T(8,128)S(1)}, u32[]{:S(2)}, u32[]{:S(2)}) collective-permute-start(f32[2,128,256]{2,1,0:T(8,128)S(1)} %get-tuple-element.66), channel_id=1, source_target_pairs={{4,0},{8,4},{12,8},{16,12},{20,16},{24,20},{28,24},{5,1},{9,5},{13... | collective-permute-start | bytes 786440 | tf_op jit(solution)/shard_map/ppermute | solution.py:21
  125.2 24.4 %collective-permute-start.18 = (f32[2,2,128,256]{3,2,1,0:T(8,128)S(1)}, f32[2,2,128,256]{3,2,1,0:T(8,128)S(1)}, u32[]{:S(2)}, u32[]{:S(2)}) collective-permute-start(f32[2,2,128,256]{3,2,1,0:T(8,128)S(1)} %pad_maximum_fusion.4), channel_id=1, source_target_pairs={{0,4},{4,8},{8,12},{12,16},{16,20},{20,24},{24,28},{1,5},{5,9},{9,... | collective-permute-start | bytes 1572872 | tf_op jit(solution)/shard_map/ppermute | solution.py:21
  127.1 26.6 %collective-permute-start.19 = (f32[2,2,128,256]{3,2,1,0:T(8,128)S(1)}, f32[2,2,128,256]{3,2,1,0:T(8,128)S(1)}, u32[]{:S(2)}, u32[]{:S(2)}) collective-permute-start(f32[2,2,128,256]{3,2,1,0:T(8,128)S(1)} %pad_maximum_fusion.3), channel_id=1, source_target_pairs={{4,0},{8,4},{12,8},{16,12},{20,16},{24,20},{28,24},{5,1},{9,5},{13... | collective-permute-start | bytes 1572872 | tf_op jit(solution)/shard_map/ppermute | solution.py:21
  132.8 21.0 %collective-permute-start.16 = (f32[2,2,512,128]{3,2,1,0:T(8,128)S(1)}, f32[2,2,512,128]{3,2,1,0:T(8,128)S(1)}, u32[]{:S(2)}, u32[]{:S(2)}) collective-permute-start(f32[2,2,512,128]{3,2,1,0:T(8,128)S(1)} %copy-done.14), channel_id=1, source_target_pairs={{0,1},{1,2},{2,3},{4,5},{5,6},{6,7},{8,9},{9,10},{10,11},{12,13},{... | collective-permute-start | bytes 3145736 | tf_op jit(solution)/shard_map/ppermute | solution.py:21
  139.7 16.1 %collective-permute-start.17 = (f32[2,2,512,128]{3,2,1,0:T(8,128)S(1)}, f32[2,2,512,128]{3,2,1,0:T(8,128)S(1)}, u32[]{:S(2)}, u32[]{:S(2)}) collective-permute-start(f32[2,2,512,128]{3,2,1,0:T(8,128)S(1)} %get-tuple-element.70), channel_id=1, source_target_pairs={{1,0},{2,1},{3,2},{5,4},{6,5},{7,6},{9,8},{10,9},{11,10},{13,12},{... | collective-permute-start | bytes 3145736 | tf_op jit(solution)/shard_map/ppermute | solution.py:21
  (11 other events, 96.2 us)
